TPU v7x, 256 devices: a whole 4x4x8 slice. The times are simulated.
256 devices in a mesh: row: 32 (over y, z), col: 8 (over x, core).
Axes of the slice: x: 4, y: 4, z: 8, core: 2. Of those that a mesh axis runs over, the one named last changes fastest.
Arguments:
- hessian: bfloat16 [8, 3328, 26624], P(None, 'row', 'col'), may hold values from -0.026001572 to 5, as said below
- exponents: int32 [26624], P(('col', 'row')), may hold values from 0 to 1
- masks: int32 [26624, 256], P(('col', 'row')), may hold values 0 or 1
- weights: bfloat16 [26624, 256], P(('col', 'row')), may hold values from -12 to 12
Outputs:
- solution_field: float32 [26624, 256], P(('col', 'row'))
- residual: float32 [26624, 256], P(('col', 'row'))
Inputs may be any that keep to these rules, and one draw needn't show every extreme that they name: `hessian`: read as an 26624 x 26624 matrix it is symmetric and positive definite.
All inputs are finite; a program needn't handle non-finite values. No bound on the sum of `masks` on one device may be relied on, other than what follows from the above.
Results may differ from a plain program's by a relative error of at most 0.014.
Values may be sent and summed in bfloat16 or wider, within the bound.
No kernel may reach another device: no remote copies, remote signals or barrier semaphores. Data moves between devices by JAX's collectives and lax.ppermute only.
A program may use at most 64 MiB of HBM per device.

v0:
```python
import jax
import jax.numpy as jnp
from jax import lax
from jax.sharding import PartitionSpec as P

ITERS = 2


def column_sums(first, second):
    return jnp.sum(first * second, axis=0)


def on_device(hessian, exponents, masks, weights):
    row_scale = jnp.exp2(-exponents.astype(jnp.float32))[:, None]
    kept = masks.astype(jnp.float32)
    dense = weights.astype(jnp.float32)

    def applied(vectors):
        rounded = (row_scale * vectors).astype(jnp.bfloat16)
        partial_sum = jnp.einsum(
            "cst,tk->csk",
            hessian,
            lax.all_gather(rounded, "row", axis=0, tiled=True),
            preferred_element_type=jnp.float32,
        )
        total = lax.psum_scatter(partial_sum, "col", scatter_dimension=0, tiled=True)[0]
        return kept * row_scale * total

    solution_field = kept * dense
    residual = applied((1.0 - kept) * dense)
    direction = residual
    norm_now = lax.psum(column_sums(residual, residual), ("row", "col"))
    for iteration in range(ITERS):
        image_now = applied(direction)
        step_size = norm_now / lax.psum(column_sums(direction, image_now), ("row", "col"))
        solution_field = solution_field + step_size * direction
        residual = residual - step_size * image_now
        if iteration + 1 < ITERS:
            fresh = lax.psum(column_sums(residual, residual), ("row", "col"))
            direction = residual + fresh / norm_now * direction
            norm_now = fresh
    return (solution_field, residual)


def solution(mesh):
    in_specs = (
        P(None, "row", "col"),
        P(("col", "row")),
        P(("col", "row"), None),
        P(("col", "row"), None),
    )
    out_specs = (P(("col", "row"), None), P(("col", "row"), None))
    return jax.shard_map(
        on_device, mesh=mesh, in_specs=in_specs, out_specs=out_specs, check_vma=False
    )
```

profile of v0, /device:TPU:32, one launch (start us, length us, event | category | flops | bytes accessed | tf_op | source)
XLA Modules:
  0.0 592.4 jit_solution(9281878398378473666)
XLA Ops:
  7.2 0.7 multiply_exponential_fusion
  7.9 1.6 fusion.18
  9.5 0.0 reduce-scatter.4.cloned.1.call-start
  9.6 80.8 %all-gather.4.cloned.1.call-done = bf16[3328,256]{1,0:T(8,128)(2,1)} async-done(((bf16[104,256]{1,0:T(8,128)(2,1)}), bf16[3328,256]{1,0:T(8,128)(2,1)}) %all-gather.4.cloned.1.call-update) | async-done | bytes 1703952 | tf_op jit(solution)/shard_map/all_gather | solution.py:23
  90.4 5.6 fusion.6
  96.0 0.0 all-gather.6.cloned.1.call-start
  96.0 32.3 %reduce-scatter.4.cloned.1.call-done = f32[1,104,256]{2,1,0:T(8,128)} async-done(((f32[8,104,256]{2,1,0:T(8,128)}), f32[1,104,256]{2,1,0:T(8,128)}) %reduce-scatter.4.cloned.1.call-update) | async-done | bytes 106512 | tf_op jit(solution)/shard_map/reduce_scatter | solution.py:26
  128.3 1.6 multiply_convert_fusion.1
  129.9 0.0 reduce-scatter.6.cloned.1.call-start
  130.0 77.3 %all-gather.6.cloned.1.call-done = bf16[3328,256]{1,0:T(8,128)(2,1)} async-done(((bf16[104,256]{1,0:T(8,128)(2,1)}), bf16[3328,256]{1,0:T(8,128)(2,1)}) %all-gather.6.cloned.1.call-update) | async-done | bytes 1703952 | tf_op jit(solution)/shard_map/all_gather | solution.py:23
  207.3 5.6 fusion.9
  212.9 0.0 all-gather.8.cloned.1.call-start
  212.9 32.3 %reduce-scatter.6.cloned.1.call-done = f32[1,104,256]{2,1,0:T(8,128)} async-done(((f32[8,104,256]{2,1,0:T(8,128)}), f32[1,104,256]{2,1,0:T(8,128)}) %reduce-scatter.6.cloned.1.call-update) | async-done | bytes 106512 | tf_op jit(solution)/shard_map/reduce_scatter | solution.py:26
  245.2 1.0 multiply_reduce_fusion.2
  246.2 76.1 %all-reduce = (f32[256]{0:T(256)S(1)}, f32[256]{0:T(256)S(1)}) all-reduce(f32[256]{0:T(256)S(1)} %get-tuple-element.3, f32[256]{0:T(256)S(1)} %get-tuple-element.2), channel_id=1, replica_groups=mesh['row'=32,'col'=8] {'row','col'}, use_global_device_ids=true, to_apply=%region_2.0 | all-reduce | flops 512 | bytes 4096 | tf_op jit(solution)/shard_map/psum | solution.py:32
  322.4 72.8 %psum.30 = f32[256]{0:T(256)S(1)} all-reduce(f32[256]{0:T(256)S(1)} %multiply_reduce_fusion.1), channel_id=1, replica_groups=mesh['row'=32,'col'=8] {'row','col'}, use_global_device_ids=true, to_apply=%region_7.0 | all-reduce | flops 256 | bytes 2048 | tf_op jit(solution)/shard_map/psum | solution.py:39
  395.2 0.7 multiply_convert_fusion
  395.9 0.0 reduce-scatter.8.cloned.1.call-start
  396.0 72.9 %all-gather.8.cloned.1.call-done = bf16[3328,256]{1,0:T(8,128)(2,1)} async-done(((bf16[104,256]{1,0:T(8,128)(2,1)}), bf16[3328,256]{1,0:T(8,128)(2,1)}) %all-gather.8.cloned.1.call-update) | async-done | bytes 1703952 | tf_op jit(solution)/shard_map/all_gather | solution.py:23
  468.9 5.6 fusion.12
  474.5 32.3 %reduce-scatter.8.cloned.1.call-done = f32[1,104,256]{2,1,0:T(8,128)} async-done(((f32[8,104,256]{2,1,0:T(8,128)}), f32[1,104,256]{2,1,0:T(8,128)}) %reduce-scatter.8.cloned.1.call-update) | async-done | bytes 106512 | tf_op jit(solution)/shard_map/reduce_scatter | solution.py:26
  506.8 1.0 multiply_reduce_fusion
  507.8 76.1 %psum.31 = f32[256]{0:T(256)S(1)} all-reduce(f32[256]{0:T(256)S(1)} %multiply_reduce_fusion), channel_id=1, replica_groups=mesh['row'=32,'col'=8] {'row','col'}, use_global_device_ids=true, to_apply=%region_10.0 | all-reduce | flops 256 | bytes 2048 | tf_op jit(solution)/shard_map/psum | solution.py:35
  584.0 1.6 multiply_subtract_fusion
  (15 shorter events, 0.2 us)
Async XLA Ops:
  7.2 83.2 %all-gather.4.cloned.1.call-start = ((), (), s32[]{:S(2)}) async-start(), calls=%async_computation.3 | async-start | bytes 1757184 | tf_op jit(solution)/shard_map/all_gather | solution.py:23
  9.5 118.8 %copy-start = (s32[104,256]{1,0:T(8,128)S(1)}, s32[104,256]{1,0:T(8,128)}, u32[]{:S(2)}) copy-start(s32[104,256]{1,0:T(8,128)} %param.6) | copy-start | bytes 319492
  9.5 118.7 %reduce-scatter.4.cloned.1.call-start = ((), (), s32[]{:S(2)}) async-start(), calls=%async_computation.4 | async-start | bytes 958464 | tf_op jit(solution)/shard_map/reduce_scatter | solution.py:26
  96.0 111.3 %all-gather.6.cloned.1.call-start = ((), (), s32[]{:S(2)}) async-start(), calls=%async_computation.5 | async-start | bytes 1757184 | tf_op jit(solution)/shard_map/all_gather | solution.py:23
  129.9 115.3 %reduce-scatter.6.cloned.1.call-start = ((), (), s32[]{:S(2)}) async-start(), calls=%async_computation.6 | async-start | bytes 958464 | tf_op jit(solution)/shard_map/reduce_scatter | solution.py:26
  212.9 256.0 %all-gather.8.cloned.1.call-start = ((), (), s32[]{:S(2)}) async-start(), calls=%async_computation.7 | async-start | bytes 1757184 | tf_op jit(solution)/shard_map/all_gather | solution.py:23
  395.9 188.0 %copy-start.1 = (bf16[104,256]{1,0:T(8,128)(2,1)S(1)}, bf16[104,256]{1,0:T(8,128)(2,1)}, u32[]{:S(2)}) copy-start(bf16[104,256]{1,0:T(8,128)(2,1)} %param.7) | copy-start | bytes 159748
  395.9 110.9 %reduce-scatter.8.cloned.1.call-start = ((), (), s32[]{:S(2)}) async-start(), calls=%async_computation.8 | async-start | bytes 958464 | tf_op jit(solution)/shard_map/reduce_scatter | solution.py:26
Sparse Core Ops, SparseCore 0:
  11.2 79.1 all-gather.3
  96.1 32.1 reduce-scatter.3
  131.8 75.4 all-gather.5
  213.0 32.1 reduce-scatter.5
  396.0 72.8 all-gather.7
  474.6 32.1 reduce-scatter.7
where the time goes:
time: 594 us; the launch traced here: 592 us
  waiting for transfers between devices  328 us (55%)
  blocking collectives  225 us (38%)
  matrix products  16.7 us (3%)
  between operations  14.1 us (2%)
  other arithmetic  8.31 us (1%)
    all_gather x3, waiting for transfers between devices, applied(): lax.all_gather(rounded, 'row', axis=0, tiled=True)  231 us
    reduce_scatter x3, waiting for transfers between devices, applied(): lax.psum_scatter(partial_sum, 'col', scatter_dimension=0, tiled=True)[0]  96.9 us
    psum x1, blocking collectives, on_device(): norm_now = lax.psum(column_sums(residual, residual), ('row', 'col'))  76.1 us
    psum x1, blocking collectives, on_device(): lax.psum(column_sums(direction, image_now), ('row', 'col'))  76.1 us
    psum x1, blocking collectives, on_device(): fresh = lax.psum(column_sums(residual, residual), ('row', 'col'))  72.8 us
    dot_general x3, matrix products, applied(): jnp.einsum('cst,tk->csk', hessian, lax.all_gather(rounded, 'row', axis=0,...  16.7 us
  transfers between devices with their start and end apart: 6, of which 6 were waited for; matrix products, arithmetic and copies ran while one was open for 0% of the time, Pallas kernels for 0%

commit v1 on v0

v1 whole, which is shorter than its diff:
```python
import jax
import jax.numpy as jnp
from jax import lax
from jax.sharding import Mesh, PartitionSpec as P

Y, Z, X, CORE = 4, 8, 4, 2
BF16, F32 = jnp.bfloat16, jnp.float32


def spread(block, axes, size):
    return lax.all_to_all(jnp.broadcast_to(block[None], (size,) + block.shape), axes, 0, 0, tiled=True)


def gather_rows(block):
    along_z = spread(block, "z", Z)
    along_z = along_z.reshape(Z * block.shape[0], block.shape[1])
    whole = spread(along_z, "y", Y)
    return whole.reshape(Y * along_z.shape[0], block.shape[1])


def scatter_rows(partial_sum):
    core = lax.axis_index("core")
    split = partial_sum.reshape((X, CORE) + partial_sum.shape[1:])
    mine = lax.dynamic_index_in_dim(split, core, 1, keepdims=False)
    other = lax.dynamic_index_in_dim(split, 1 - core, 1, keepdims=False)
    half = mine + lax.ppermute(other, "core", [(0, 1), (1, 0)])
    return jnp.sum(lax.all_to_all(half, "x", 0, 0, tiled=True), axis=0)


def total_sums(sums):
    sums = jnp.sum(spread(sums, ("x", "core"), X * CORE), axis=0)
    return jnp.sum(spread(sums, ("y", "z"), Y * Z), axis=0)


def stack_sums(*rows):
    zero = jnp.zeros_like(rows[0])
    return jnp.stack(list(rows) + [zero] * (8 - len(rows)))


def column_sums(first, second):
    return jnp.sum(first * second, axis=0)


def on_device(hessian, exponents, masks, weights):
    row_scale = jnp.exp2(-exponents.astype(F32))[:, None]
    kept = masks.astype(F32)
    dense = weights.astype(F32)

    def applied(vectors):
        rounded = (row_scale * vectors).astype(BF16)
        partial_sum = jnp.einsum("cst,tk->csk", hessian, gather_rows(rounded), preferred_element_type=F32)
        return kept * row_scale * scatter_rows(partial_sum)

    solution_field = kept * dense
    first = applied((1.0 - kept) * dense)
    image = applied(first)
    sums = total_sums(
        stack_sums(column_sums(first, first), column_sums(first, image), column_sums(image, image))
    )
    norm, along, square = sums[0], sums[1], sums[2]
    step = norm / along
    residual = first - step * image
    fresh = norm - 2.0 * step * along + step * step * square
    direction = residual + fresh / norm * first
    solution_field = solution_field + step * first
    image = applied(direction)
    sums = total_sums(stack_sums(column_sums(direction, image)))
    step = fresh / sums[0]
    return (solution_field + step * direction, residual - step * image)


def solution(mesh):
    fine = Mesh(mesh.devices.reshape(Y, Z, X, CORE), ("y", "z", "x", "core"))
    owner = ("x", "core", "y", "z")
    in_specs = (
        P(None, ("y", "z"), ("x", "core")),
        P(owner),
        P(owner, None),
        P(owner, None),
    )
    out_specs = (P(owner, None), P(owner, None))
    return jax.shard_map(on_device, mesh=fine, in_specs=in_specs, out_specs=out_specs, check_vma=False)
```

time: 594 us -> 239 us (0.40)
  waiting for transfers between devices: 328 us -> 34.5 us
  blocking collectives: 225 us -> 176 us
  between operations: 14.1 us -> 0.88 us
  starting transfers between devices: 0.25 us -> 8.33 us
    all_gather x3 -> x0, waiting for transfers between devices: 231 us -> none  [applied(): lax.all_gather(rounded, 'row', axis=0, tiled=True)]
    psum x3 -> x0, blocking collectives: 225 us -> none  [the longest x1 76.1 us: on_device(): norm_now = lax.psum(column_sums(residual, residual), ('row', 'col'))]
    all_to_all x0 -> x11, blocking collectives: none -> 176 us  [the longest x9 152 us: spread(): lax.all_to_all(jnp.broadcast_to(block[None], (size,) + block.shape), axes...]
    reduce_scatter x3 -> x0, waiting for transfers between devices: 96.9 us -> none  [applied(): lax.psum_scatter(partial_sum, 'col', scatter_dimension=0, tiled=True)[0]]
    all_to_all x0 -> x2, waiting for transfers between devices: none -> 29.2 us  [the longest x1 20.3 us: spread(): lax.all_to_all(jnp.broadcast_to(block[None], (size,) + block.shape), axes...]
    all_to_all x0 -> x2, starting transfers between devices: none -> 8.06 us  [the longest x1 4.46 us: spread(): lax.all_to_all(jnp.broadcast_to(block[None], (size,) + block.shape), axes...]
  transfers between devices with their start and end apart: 6 -> 5, of which waited for: 6 -> 5; matrix products, arithmetic and copies ran while one was open for 0% -> 0% of each run, Pallas kernels for 0% -> 0%
where the time goes in v1:
time: 239 us; the launch traced here: 238 us
  blocking collectives  176 us (74%)
  waiting for transfers between devices  34.5 us (14%)
  matrix products  12.5 us (5%)
  starting transfers between devices  8.33 us (3%)
  other arithmetic  4.03 us (2%)
    all_to_all x9, blocking collectives, spread(): lax.all_to_all(jnp.broadcast_to(block[None], (size,) + block.shape), axes...  152 us
    all_to_all x2, blocking collectives, scatter_rows(): return jnp.sum(lax.all_to_all(half, 'x', 0, 0, tiled=True), axis=0)  24.2 us
    all_to_all x1, waiting for transfers between devices, spread(): lax.all_to_all(jnp.broadcast_to(block[None], (size,) + block.shape), axes...  20.3 us
    dot_general x3, matrix products, applied(): jnp.einsum('cst,tk->csk', hessian, gather_rows(rounded), preferred_elemen...  12.5 us
    all_to_all x1, waiting for transfers between devices, scatter_rows(): return jnp.sum(lax.all_to_all(half, 'x', 0, 0, tiled=True), axis=0)  8.87 us
    ppermute x3, waiting for transfers between devices, scatter_rows(): half = mine + lax.ppermute(other, 'core', [(0, 1), (1, 0)])  5.27 us
  transfers between devices with their start and end apart: 5, of which 5 were waited for; matrix products, arithmetic and copies ran while one was open for 0% of the time, Pallas kernels for 0%

profile of v1, /device:TPU:32, one launch (start us, length us, event | category | flops | bytes accessed | tf_op | source)
XLA Modules:
  0.0 238.1 jit_solution(9754557266878789808)
XLA Ops:
  1.3 1.0 fusion.3
  2.3 22.3 %all_to_all.65 = bf16[8,104,256]{2,1,0:T(8,128)(2,1)S(1)} all-to-all(bf16[8,104,256]{2,1,0:T(8,128)(2,1)S(1)} %broadcast_in_dim.26), channel_id=1, replica_groups=mesh['y'=4,'z'=8,'x'=4,'core'=2] {'z'}, dimensions={0} | all-to-all | bytes 851968 | tf_op jit(solution)/shard_map/all_to_all | solution.py:11
  24.6 1.3 broadcast_in_dim.28
  25.9 4.5 %all-to-all-start.1 = ((bf16[4,832,256]{2,1,0:T(8,128)(2,1)}), bf16[4,832,256]{2,1,0:T(8,128)(2,1)S(1)}, u32[]{:S(2)}, u32[]{:S(2)}) async-start(bf16[4,832,256]{2,1,0:T(8,128)(2,1)} %broadcast_in_dim.28), calls=%async_computation.1 | async-start | bytes 3407872 | tf_op jit(solution)/shard_map/all_to_all | solution.py:11
  30.4 20.3 %all-to-all-done.1 = bf16[4,832,256]{2,1,0:T(8,128)(2,1)S(1)} async-done(((bf16[4,832,256]{2,1,0:T(8,128)(2,1)}), bf16[4,832,256]{2,1,0:T(8,128)(2,1)S(1)}, u32[]{:S(2)}, u32[]{:S(2)}) %all-to-all-start.1) | async-done | bytes 1703968 | tf_op jit(solution)/shard_map/all_to_all | solution.py:11
  50.7 4.2 %fusion.11 = f32[256,8,104]{0,2,1:T(8,128)S(1)} fusion(bf16[3328,256,1]{1,0,2:T(8,128)(2,1)S(1)} %bitcast.46, bf16[8,104,3328]{2,1,0:T(8,128)(2,1)} %param.4), kind=kOutput, calls=%fused_computation.32 | convolution fusion | flops 1417674752 | bytes 8093696 | tf_op jit(solution)/shard_map/cst,tk->csk/dot_general | solution.py:51
  55.1 1.8 collective-permute-done
  56.9 12.8 %all_to_all.66 = f32[4,104,256]{2,1,0:T(8,128)S(1)} all-to-all(f32[4,104,256]{2,1,0:T(8,128)S(1)} %bitcast_add_fusion.2), channel_id=1, replica_groups=mesh['y'=4,'z'=8,'x'=4,'core'=2] {'x'}, dimensions={0} | all-to-all | bytes 851968 | tf_op jit(solution)/shard_map/all_to_all | solution.py:27
  69.9 17.6 %all_to_all.67 = bf16[8,104,256]{2,1,0:T(8,128)(2,1)S(1)} all-to-all(bf16[8,104,256]{2,1,0:T(8,128)(2,1)S(1)} %broadcast_in_dim.29), channel_id=1, replica_groups=mesh['y'=4,'z'=8,'x'=4,'core'=2] {'z'}, dimensions={0} | all-to-all | bytes 851968 | tf_op jit(solution)/shard_map/all_to_all | solution.py:11
  87.6 21.9 %all_to_all.68 = bf16[4,832,256]{2,1,0:T(8,128)(2,1)S(1)} all-to-all(bf16[4,832,256]{2,1,0:T(8,128)(2,1)S(1)} %broadcast_in_dim.31), channel_id=1, replica_groups=mesh['y'=4,'z'=8,'x'=4,'core'=2] {'y'}, dimensions={0} | all-to-all | bytes 3407872 | tf_op jit(solution)/shard_map/all_to_all | solution.py:11
  109.6 4.2 %fusion.12 = f32[256,8,104]{0,2,1:T(8,128)S(1)} fusion(bf16[3328,256,1]{1,0,2:T(8,128)(2,1)S(1)} %bitcast.47, bf16[8,104,3328]{2,1,0:T(8,128)(2,1)} %param.4), kind=kOutput, calls=%fused_computation.33 | convolution fusion | flops 1417674752 | bytes 8093696 | tf_op jit(solution)/shard_map/cst,tk->csk/dot_general | solution.py:51
  113.9 1.8 collective-permute-done.1
  115.7 11.4 %all_to_all.69 = f32[4,104,256]{2,1,0:T(8,128)S(1)} all-to-all(f32[4,104,256]{2,1,0:T(8,128)S(1)} %bitcast_add_fusion.1), channel_id=1, replica_groups=mesh['y'=4,'z'=8,'x'=4,'core'=2] {'x'}, dimensions={0} | all-to-all | bytes 851968 | tf_op jit(solution)/shard_map/all_to_all | solution.py:27
  127.3 8.0 %all_to_all.70 = f32[8,8,256]{2,1,0:T(8,128)S(1)} all-to-all(f32[8,8,256]{2,1,0:T(8,128)S(1)} %broadcast_in_dim.32), channel_id=1, replica_groups=mesh['y'=4,'z'=8,'x'=4,'core'=2] {'x','core'}, dimensions={0} | all-to-all | bytes 131072 | tf_op jit(solution)/shard_map/all_to_all | solution.py:11
  135.3 18.1 %all_to_all.71 = f32[32,8,256]{2,1,0:T(8,128)S(1)} all-to-all(f32[32,8,256]{2,1,0:T(8,128)S(1)} %broadcast_in_dim.33), channel_id=1, replica_groups=mesh['y'=4,'z'=8,'x'=4,'core'=2] {'y','z'}, dimensions={0} | all-to-all | bytes 524288 | tf_op jit(solution)/shard_map/all_to_all | solution.py:11
  153.6 15.9 %all_to_all.72 = bf16[8,104,256]{2,1,0:T(8,128)(2,1)S(1)} all-to-all(bf16[8,104,256]{2,1,0:T(8,128)(2,1)S(1)} %broadcast_in_dim.34), channel_id=1, replica_groups=mesh['y'=4,'z'=8,'x'=4,'core'=2] {'z'}, dimensions={0} | all-to-all | bytes 851968 | tf_op jit(solution)/shard_map/all_to_all | solution.py:11
  169.7 21.5 %all_to_all.73 = bf16[4,832,256]{2,1,0:T(8,128)(2,1)S(1)} all-to-all(bf16[4,832,256]{2,1,0:T(8,128)(2,1)S(1)} %broadcast_in_dim.36), channel_id=1, replica_groups=mesh['y'=4,'z'=8,'x'=4,'core'=2] {'y'}, dimensions={0} | all-to-all | bytes 3407872 | tf_op jit(solution)/shard_map/all_to_all | solution.py:11
  191.2 4.2 %fusion.13 = f32[256,8,104]{0,2,1:T(8,128)S(1)} fusion(bf16[3328,256,1]{1,0,2:T(8,128)(2,1)S(1)} %bitcast.48, bf16[8,104,3328]{2,1,0:T(8,128)(2,1)} %param.4), kind=kOutput, calls=%fused_computation.34 | convolution fusion | flops 1417674752 | bytes 8093696 | tf_op jit(solution)/shard_map/cst,tk->csk/dot_general | solution.py:51
  195.5 1.8 collective-permute-done.2
  197.3 0.8 bitcast_add_fusion
  198.1 3.6 %all-to-all-start.10 = ((f32[4,104,256]{2,1,0:T(8,128)}), f32[4,104,256]{2,1,0:T(8,128)S(1)}, u32[]{:S(2)}, u32[]{:S(2)}) async-start(f32[4,104,256]{2,1,0:T(8,128)} %bitcast_add_fusion), calls=%async_computation.10 | async-start | bytes 851968 | tf_op jit(solution)/shard_map/all_to_all | solution.py:27
  201.8 8.9 %all-to-all-done.10 = f32[4,104,256]{2,1,0:T(8,128)S(1)} async-done(((f32[4,104,256]{2,1,0:T(8,128)}), f32[4,104,256]{2,1,0:T(8,128)S(1)}, u32[]{:S(2)}, u32[]{:S(2)}) %all-to-all-start.10) | async-done | bytes 426016 | tf_op jit(solution)/shard_map/all_to_all | solution.py:27
  210.9 8.0 %all_to_all.74 = f32[8,8,256]{2,1,0:T(8,128)S(1)} all-to-all(f32[8,8,256]{2,1,0:T(8,128)S(1)} %broadcast_in_dim.37), channel_id=1, replica_groups=mesh['y'=4,'z'=8,'x'=4,'core'=2] {'x','core'}, dimensions={0} | all-to-all | bytes 131072 | tf_op jit(solution)/shard_map/all_to_all | solution.py:11
  218.9 18.4 %all_to_all.75 = f32[32,8,256]{2,1,0:T(8,128)S(1)} all-to-all(f32[32,8,256]{2,1,0:T(8,128)S(1)} %broadcast_in_dim.38), channel_id=1, replica_groups=mesh['y'=4,'z'=8,'x'=4,'core'=2] {'y','z'}, dimensions={0} | all-to-all | bytes 524288 | tf_op jit(solution)/shard_map/all_to_all | solution.py:11
  (42 shorter events, 3.1 us)
Async XLA Ops:
  25.9 24.8 %all-to-all-start.1 = ((bf16[4,832,256]{2,1,0:T(8,128)(2,1)}), bf16[4,832,256]{2,1,0:T(8,128)(2,1)S(1)}, u32[]{:S(2)}, u32[]{:S(2)}) async-start(bf16[4,832,256]{2,1,0:T(8,128)(2,1)} %broadcast_in_dim.28), calls=%async_computation.1 | async-start | bytes 3407872 | tf_op jit(solution)/shard_map/all_to_all | solution.py:11
  54.9 14.8 %copy-start = (s32[104,256]{1,0:T(8,128)S(1)}, s32[104,256]{1,0:T(8,128)}, u32[]{:S(2)}) copy-start(s32[104,256]{1,0:T(8,128)} %param.6) | copy-start | bytes 319492
  55.0 1.9 collective-permute-start
  113.8 1.9 collective-permute-start.1
  195.4 1.9 collective-permute-start.2
  198.1 39.3 %copy-start.1 = (bf16[104,256]{1,0:T(8,128)(2,1)S(1)}, bf16[104,256]{1,0:T(8,128)(2,1)}, u32[]{:S(2)}) copy-start(bf16[104,256]{1,0:T(8,128)(2,1)} %param.7) | copy-start | bytes 159748
  198.1 12.6 %all-to-all-start.10 = ((f32[4,104,256]{2,1,0:T(8,128)}), f32[4,104,256]{2,1,0:T(8,128)S(1)}, u32[]{:S(2)}, u32[]{:S(2)}) async-start(f32[4,104,256]{2,1,0:T(8,128)} %bitcast_add_fusion), calls=%async_computation.10 | async-start | bytes 851968 | tf_op jit(solution)/shard_map/all_to_all | solution.py:27

commit v2 on v1

--- a/solution.py
+++ b/solution.py
@@ -11,20 +11,33 @@
     return lax.all_to_all(jnp.broadcast_to(block[None], (size,) + block.shape), axes, 0, 0, tiled=True)
 
 
+def moved(block, axis, size, shift):
+    return lax.ppermute(block, axis, [(i, (i + shift) % size) for i in range(size)])
+
+
 def gather_rows(block):
     along_z = spread(block, "z", Z)
     along_z = along_z.reshape(Z * block.shape[0], block.shape[1])
-    whole = spread(along_z, "y", Y)
+    place = lax.axis_index("y")
+    received = [moved(along_z, "y", Y, shift) for shift in (2, 1, 3)]
+    whole = jnp.zeros((Y,) + along_z.shape, block.dtype)
+    whole = lax.dynamic_update_index_in_dim(whole, along_z, place, 0)
+    for shift, piece in zip((2, 1, 3), received):
+        whole = lax.dynamic_update_index_in_dim(whole, piece, (place + Y - shift) % Y, 0)
     return whole.reshape(Y * along_z.shape[0], block.shape[1])
 
 
 def scatter_rows(partial_sum):
     core = lax.axis_index("core")
+    place = lax.axis_index("x")
     split = partial_sum.reshape((X, CORE) + partial_sum.shape[1:])
     mine = lax.dynamic_index_in_dim(split, core, 1, keepdims=False)
     other = lax.dynamic_index_in_dim(split, 1 - core, 1, keepdims=False)
     half = mine + lax.ppermute(other, "core", [(0, 1), (1, 0)])
-    return jnp.sum(lax.all_to_all(half, "x", 0, 0, tiled=True), axis=0)
+    total = lax.dynamic_index_in_dim(half, place, 0, keepdims=False)
+    for shift in (2, 1, 3):
+        total = total + moved(lax.dynamic_index_in_dim(half, (place + shift) % X, 0, keepdims=False), "x", X, shift)
+    return total
 
 
 def total_sums(sums):

time: 239 us -> 221 us (0.925)
  blocking collectives: 176 us -> 112 us
  starting transfers between devices: 8.33 us -> 33.2 us
  waiting for transfers between devices: 34.5 us -> 57.6 us
    ppermute x0 -> x18, waiting for transfers between devices: none -> 52.4 us  [moved(): lax.ppermute(block, axis, [(i, (i + shift) % size) for i in range(size)])]
    all_to_all x9 -> x7, blocking collectives: 152 us -> 112 us  [spread(): lax.all_to_all(jnp.broadcast_to(block[None], (size,) + block.shape), axes...]
    ppermute x0 -> x18, starting transfers between devices: none -> 32.9 us  [moved(): lax.ppermute(block, axis, [(i, (i + shift) % size) for i in range(size)])]
    all_to_all x2 -> x0, waiting for transfers between devices: 29.2 us -> none  [the longest x1 20.3 us: spread(): lax.all_to_all(jnp.broadcast_to(block[None], (size,) + block.shape), axes...]
    all_to_all x2 -> x0, blocking collectives: 24.2 us -> none  [scatter_rows(): return jnp.sum(lax.all_to_all(half, 'x', 0, 0, tiled=True), axis=0)]
    all_to_all x2 -> x0, starting transfers between devices: 8.06 us -> none  [the longest x1 4.46 us: spread(): lax.all_to_all(jnp.broadcast_to(block[None], (size,) + block.shape), axes...]
  transfers between devices with their start and end apart: 5 -> 21, of which waited for: 5 -> 16; matrix products, arithmetic and copies ran while one was open for 0% -> 0% of each run, Pallas kernels for 0% -> 0%
where the time goes in v2:
time: 221 us
  blocking collectives  112 us (51%)
  waiting for transfers between devices  57.6 us (26%)
  starting transfers between devices  33.2 us (15%)
  matrix products  12.6 us (6%)
  other arithmetic  3.21 us (1%)
    all_to_all x7, blocking collectives, spread(): lax.all_to_all(jnp.broadcast_to(block[None], (size,) + block.shape), axes...  112 us
    ppermute x18, waiting for transfers between devices, moved(): lax.ppermute(block, axis, [(i, (i + shift) % size) for i in range(size)])  52.4 us
    ppermute x18, starting transfers between devices, moved(): lax.ppermute(block, axis, [(i, (i + shift) % size) for i in range(size)])  32.9 us
    dot_general x3, matrix products, applied(): jnp.einsum('cst,tk->csk', hessian, gather_rows(rounded), preferred_elemen...  12.6 us
    ppermute x3, waiting for transfers between devices, scatter_rows(): half = mine + lax.ppermute(other, 'core', [(0, 1), (1, 0)])  5.22 us
  transfers between devices with their start and end apart: 21, of which 16 were waited for; matrix products, arithmetic and copies ran while one was open for 0% of the time, Pallas kernels for 0%

profile of v2, /device:TPU:32, one launch (start us, length us, event | category | flops | bytes accessed | tf_op | source)
XLA Modules:
  0.0 220.9 jit_solution(9054817246930600198)
XLA Ops:
  2.3 22.3 %all_to_all.35 = bf16[8,104,256]{2,1,0:T(8,128)(2,1)S(1)} all-to-all(bf16[8,104,256]{2,1,0:T(8,128)(2,1)S(1)} %broadcast_in_dim.85), channel_id=1, replica_groups=mesh['y'=4,'z'=8,'x'=4,'core'=2] {'z'}, dimensions={0} | all-to-all | bytes 851968 | tf_op jit(solution)/shard_map/all_to_all | solution.py:11
  24.6 3.2 %collective-permute-start = (bf16[832,256]{1,0:T(8,128)(2,1)S(1)}, bf16[832,256]{1,0:T(8,128)(2,1)S(1)}, u32[]{:S(2)}, u32[]{:S(2)}) collective-permute-start(bf16[832,256]{1,0:T(8,128)(2,1)S(1)} %bitcast.121), channel_id=1, source_target_pairs={{0,128},{64,192},{128,0},{192,64},{1,129},{65,193},{129,1},{193,65... | collective-permute-start | bytes 1277960 | tf_op jit(solution)/shard_map/ppermute | solution.py:15
  28.5 2.6 %collective-permute-start.2 = (bf16[832,256]{1,0:T(8,128)(2,1)S(1)}, bf16[832,256]{1,0:T(8,128)(2,1)S(1)}, u32[]{:S(2)}, u32[]{:S(2)}) collective-permute-start(bf16[832,256]{1,0:T(8,128)(2,1)S(1)} %bitcast.123), channel_id=1, source_target_pairs={{0,192},{64,0},{128,64},{192,128},{1,193},{65,1},{129,65},{193,129... | collective-permute-start | bytes 1277960 | tf_op jit(solution)/shard_map/ppermute | solution.py:15
  31.2 7.7 %collective-permute-done = bf16[832,256]{1,0:T(8,128)(2,1)S(1)} collective-permute-done((bf16[832,256]{1,0:T(8,128)(2,1)S(1)}, bf16[832,256]{1,0:T(8,128)(2,1)S(1)}, u32[]{:S(2)}, u32[]{:S(2)}) %collective-permute-start) | collective-permute-done | bytes 426016 | tf_op jit(solution)/shard_map/ppermute | solution.py:15
  39.0 6.1 %collective-permute-done.1 = bf16[832,256]{1,0:T(8,128)(2,1)S(1)} collective-permute-done((bf16[832,256]{1,0:T(8,128)(2,1)S(1)}, bf16[832,256]{1,0:T(8,128)(2,1)S(1)}, u32[]{:S(2)}, u32[]{:S(2)}) %collective-permute-start.1) | collective-permute-done | bytes 426016 | tf_op jit(solution)/shard_map/ppermute | solution.py:15
  45.5 4.2 %fusion.18 = f32[256,8,104]{0,2,1:T(8,128)S(1)} fusion(bf16[3328,256,1]{1,0,2:T(8,128)(2,1)S(1)} %bitcast.119, bf16[8,104,3328]{2,1,0:T(8,128)(2,1)} %param.4), kind=kOutput, calls=%fused_computation.62 | convolution fusion | flops 1417674752 | bytes 8093696 | tf_op jit(solution)/shard_map/cst,tk->csk/dot_general | solution.py:64
  51.7 3.1 %collective-permute-start.4 = (f32[104,256]{1,0:T(8,128)S(1)}, f32[104,256]{1,0:T(8,128)S(1)}, u32[]{:S(2)}, u32[]{:S(2)}) collective-permute-start(f32[104,256]{1,0:T(8,128)S(1)} %get-tuple-element.19), channel_id=1, source_target_pairs={{0,4},{2,6},{4,0},{6,2},{1,5},{3,7},{5,1},{7,3},{8,12},{10,14},{12... | collective-permute-start | bytes 319496 | tf_op jit(solution)/shard_map/ppermute | solution.py:15
  55.4 2.6 %collective-permute-start.6 = (f32[104,256]{1,0:T(8,128)S(1)}, f32[104,256]{1,0:T(8,128)S(1)}, u32[]{:S(2)}, u32[]{:S(2)}) collective-permute-start(f32[104,256]{1,0:T(8,128)S(1)} %get-tuple-element.20), channel_id=1, source_target_pairs={{0,6},{2,0},{4,2},{6,4},{1,7},{3,1},{5,3},{7,5},{8,14},{10,8},{12,... | collective-permute-start | bytes 319496 | tf_op jit(solution)/shard_map/ppermute | solution.py:15
  61.0 17.8 %all_to_all.36 = bf16[8,104,256]{2,1,0:T(8,128)(2,1)S(1)} all-to-all(bf16[8,104,256]{2,1,0:T(8,128)(2,1)S(1)} %broadcast_in_dim.90), channel_id=1, replica_groups=mesh['y'=4,'z'=8,'x'=4,'core'=2] {'z'}, dimensions={0} | all-to-all | bytes 851968 | tf_op jit(solution)/shard_map/all_to_all | solution.py:11
  84.3 8.8 %collective-permute-done.7 = bf16[832,256]{1,0:T(8,128)(2,1)S(1)} collective-permute-done((bf16[832,256]{1,0:T(8,128)(2,1)S(1)}, bf16[832,256]{1,0:T(8,128)(2,1)S(1)}, u32[]{:S(2)}, u32[]{:S(2)}) %collective-permute-start.7) | collective-permute-done | bytes 426016 | tf_op jit(solution)/shard_map/ppermute | solution.py:15
  93.1 5.5 %collective-permute-done.8 = bf16[832,256]{1,0:T(8,128)(2,1)S(1)} collective-permute-done((bf16[832,256]{1,0:T(8,128)(2,1)S(1)}, bf16[832,256]{1,0:T(8,128)(2,1)S(1)}, u32[]{:S(2)}, u32[]{:S(2)}) %collective-permute-start.8) | collective-permute-done | bytes 426016 | tf_op jit(solution)/shard_map/ppermute | solution.py:15
  98.6 4.2 %fusion.19 = f32[256,8,104]{0,2,1:T(8,128)S(1)} fusion(bf16[3328,256,1]{1,0,2:T(8,128)(2,1)S(1)} %bitcast.120, bf16[8,104,3328]{2,1,0:T(8,128)(2,1)} %param.4), kind=kOutput, calls=%fused_computation.63 | convolution fusion | flops 1417674752 | bytes 8093696 | tf_op jit(solution)/shard_map/cst,tk->csk/dot_general | solution.py:64
  104.9 2.3 %collective-permute-start.11 = (f32[104,256]{1,0:T(8,128)S(1)}, f32[104,256]{1,0:T(8,128)S(1)}, u32[]{:S(2)}, u32[]{:S(2)}) collective-permute-start(f32[104,256]{1,0:T(8,128)S(1)} %get-tuple-element.16), channel_id=1, source_target_pairs={{0,4},{2,6},{4,0},{6,2},{1,5},{3,7},{5,1},{7,3},{8,12},{10,14},{12... | collective-permute-start | bytes 319496 | tf_op jit(solution)/shard_map/ppermute | solution.py:15
  107.9 2.6 %collective-permute-start.13 = (f32[104,256]{1,0:T(8,128)S(1)}, f32[104,256]{1,0:T(8,128)S(1)}, u32[]{:S(2)}, u32[]{:S(2)}) collective-permute-start(f32[104,256]{1,0:T(8,128)S(1)} %get-tuple-element.17), channel_id=1, source_target_pairs={{0,6},{2,0},{4,2},{6,4},{1,7},{3,1},{5,3},{7,5},{8,14},{10,8},{12,... | collective-permute-start | bytes 319496 | tf_op jit(solution)/shard_map/ppermute | solution.py:15
  114.1 10.0 %all_to_all.37 = f32[8,8,256]{2,1,0:T(8,128)S(1)} all-to-all(f32[8,8,256]{2,1,0:T(8,128)S(1)} %broadcast_in_dim.95), channel_id=1, replica_groups=mesh['y'=4,'z'=8,'x'=4,'core'=2] {'x','core'}, dimensions={0} | all-to-all | bytes 131072 | tf_op jit(solution)/shard_map/all_to_all | solution.py:11
  124.1 18.9 %all_to_all.38 = f32[32,8,256]{2,1,0:T(8,128)S(1)} all-to-all(f32[32,8,256]{2,1,0:T(8,128)S(1)} %broadcast_in_dim.96), channel_id=1, replica_groups=mesh['y'=4,'z'=8,'x'=4,'core'=2] {'y','z'}, dimensions={0} | all-to-all | bytes 524288 | tf_op jit(solution)/shard_map/all_to_all | solution.py:11
  143.2 15.9 %all_to_all.39 = bf16[8,104,256]{2,1,0:T(8,128)(2,1)S(1)} all-to-all(bf16[8,104,256]{2,1,0:T(8,128)(2,1)S(1)} %broadcast_in_dim.97), channel_id=1, replica_groups=mesh['y'=4,'z'=8,'x'=4,'core'=2] {'z'}, dimensions={0} | all-to-all | bytes 851968 | tf_op jit(solution)/shard_map/all_to_all | solution.py:11
  161.2 2.8 %collective-permute-start.16 = (bf16[832,256]{1,0:T(8,128)(2,1)S(1)}, bf16[832,256]{1,0:T(8,128)(2,1)S(1)}, u32[]{:S(2)}, u32[]{:S(2)}) collective-permute-start(bf16[832,256]{1,0:T(8,128)(2,1)S(1)} %bitcast.127), channel_id=1, source_target_pairs={{0,192},{64,0},{128,64},{192,128},{1,193},{65,1},{129,65},{193,129... | collective-permute-start | bytes 1277960 | tf_op jit(solution)/shard_map/ppermute | solution.py:15
  164.1 8.8 %collective-permute-done.14 = bf16[832,256]{1,0:T(8,128)(2,1)S(1)} collective-permute-done((bf16[832,256]{1,0:T(8,128)(2,1)S(1)}, bf16[832,256]{1,0:T(8,128)(2,1)S(1)}, u32[]{:S(2)}, u32[]{:S(2)}) %collective-permute-start.14) | collective-permute-done | bytes 426016 | tf_op jit(solution)/shard_map/ppermute | solution.py:15
  172.9 4.4 %collective-permute-done.15 = bf16[832,256]{1,0:T(8,128)(2,1)S(1)} collective-permute-done((bf16[832,256]{1,0:T(8,128)(2,1)S(1)}, bf16[832,256]{1,0:T(8,128)(2,1)S(1)}, u32[]{:S(2)}, u32[]{:S(2)}) %collective-permute-start.15) | collective-permute-done | bytes 426016 | tf_op jit(solution)/shard_map/ppermute | solution.py:15
  177.4 4.2 %fusion.20 = f32[256,8,104]{0,2,1:T(8,128)S(1)} fusion(bf16[3328,256,1]{1,0,2:T(8,128)(2,1)S(1)} %bitcast.118, bf16[8,104,3328]{2,1,0:T(8,128)(2,1)} %param.4), kind=kOutput, calls=%fused_computation.64 | convolution fusion | flops 1417674752 | bytes 8093696 | tf_op jit(solution)/shard_map/cst,tk->csk/dot_general | solution.py:64
  188.1 3.0 %collective-permute-done.18 = f32[104,256]{1,0:T(8,128)S(1)} collective-permute-done((f32[104,256]{1,0:T(8,128)S(1)}, f32[104,256]{1,0:T(8,128)S(1)}, u32[]{:S(2)}, u32[]{:S(2)}) %collective-permute-start.18) | collective-permute-done | bytes 106528 | tf_op jit(solution)/shard_map/ppermute | solution.py:15
  192.7 8.2 %all_to_all.40 = f32[8,8,256]{2,1,0:T(8,128)S(1)} all-to-all(f32[8,8,256]{2,1,0:T(8,128)S(1)} %broadcast_in_dim.102), channel_id=1, replica_groups=mesh['y'=4,'z'=8,'x'=4,'core'=2] {'x','core'}, dimensions={0} | all-to-all | bytes 131072 | tf_op jit(solution)/shard_map/all_to_all | solution.py:11
  201.0 19.1 %all_to_all.41 = f32[32,8,256]{2,1,0:T(8,128)S(1)} all-to-all(f32[32,8,256]{2,1,0:T(8,128)S(1)} %broadcast_in_dim.103), channel_id=1, replica_groups=mesh['y'=4,'z'=8,'x'=4,'core'=2] {'y','z'}, dimensions={0} | all-to-all | bytes 524288 | tf_op jit(solution)/shard_map/all_to_all | solution.py:11
  (82 shorter events, 31.7 us)
Async XLA Ops:
  24.6 14.3 %collective-permute-start = (bf16[832,256]{1,0:T(8,128)(2,1)S(1)}, bf16[832,256]{1,0:T(8,128)(2,1)S(1)}, u32[]{:S(2)}, u32[]{:S(2)}) collective-permute-start(bf16[832,256]{1,0:T(8,128)(2,1)S(1)} %bitcast.121), channel_id=1, source_target_pairs={{0,128},{64,192},{128,0},{192,64},{1,129},{65,193},{129,1},{193,65... | collective-permute-start | bytes 1277960 | tf_op jit(solution)/shard_map/ppermute | solution.py:15
  27.8 17.2 %collective-permute-start.1 = (bf16[832,256]{1,0:T(8,128)(2,1)S(1)}, bf16[832,256]{1,0:T(8,128)(2,1)S(1)}, u32[]{:S(2)}, u32[]{:S(2)}) collective-permute-start(bf16[832,256]{1,0:T(8,128)(2,1)S(1)} %bitcast.122), channel_id=1, source_target_pairs={{0,64},{64,128},{128,192},{192,0},{1,65},{65,129},{129,193},{193,1... | collective-permute-start | bytes 1277960 | tf_op jit(solution)/shard_map/ppermute | solution.py:15
  28.5 16.9 %collective-permute-start.2 = (bf16[832,256]{1,0:T(8,128)(2,1)S(1)}, bf16[832,256]{1,0:T(8,128)(2,1)S(1)}, u32[]{:S(2)}, u32[]{:S(2)}) collective-permute-start(bf16[832,256]{1,0:T(8,128)(2,1)S(1)} %bitcast.123), channel_id=1, source_target_pairs={{0,192},{64,0},{128,64},{192,128},{1,193},{65,1},{129,65},{193,129... | collective-permute-start | bytes 1277960 | tf_op jit(solution)/shard_map/ppermute | solution.py:15
  49.7 11.2 %copy-start = (s32[104,256]{1,0:T(8,128)S(1)}, s32[104,256]{1,0:T(8,128)}, u32[]{:S(2)}) copy-start(s32[104,256]{1,0:T(8,128)} %param.6) | copy-start | bytes 319492
  49.7 1.9 collective-permute-start.3
  51.7 7.1 %collective-permute-start.4 = (f32[104,256]{1,0:T(8,128)S(1)}, f32[104,256]{1,0:T(8,128)S(1)}, u32[]{:S(2)}, u32[]{:S(2)}) collective-permute-start(f32[104,256]{1,0:T(8,128)S(1)} %get-tuple-element.19), channel_id=1, source_target_pairs={{0,4},{2,6},{4,0},{6,2},{1,5},{3,7},{5,1},{7,3},{8,12},{10,14},{12... | collective-permute-start | bytes 319496 | tf_op jit(solution)/shard_map/ppermute | solution.py:15
  54.8 6.1 %collective-permute-start.5 = (f32[104,256]{1,0:T(8,128)S(1)}, f32[104,256]{1,0:T(8,128)S(1)}, u32[]{:S(2)}, u32[]{:S(2)}) collective-permute-start(f32[104,256]{1,0:T(8,128)S(1)} %get-tuple-element.21), channel_id=1, source_target_pairs={{0,2},{2,4},{4,6},{6,0},{1,3},{3,5},{5,7},{7,1},{8,10},{10,12},{12... | collective-permute-start | bytes 319496 | tf_op jit(solution)/shard_map/ppermute | solution.py:15
  55.4 5.5 %collective-permute-start.6 = (f32[104,256]{1,0:T(8,128)S(1)}, f32[104,256]{1,0:T(8,128)S(1)}, u32[]{:S(2)}, u32[]{:S(2)}) collective-permute-start(f32[104,256]{1,0:T(8,128)S(1)} %get-tuple-element.20), channel_id=1, source_target_pairs={{0,6},{2,0},{4,2},{6,4},{1,7},{3,1},{5,3},{7,5},{8,14},{10,8},{12,... | collective-permute-start | bytes 319496 | tf_op jit(solution)/shard_map/ppermute | solution.py:15
  78.8 14.3 %collective-permute-start.7 = (bf16[832,256]{1,0:T(8,128)(2,1)S(1)}, bf16[832,256]{1,0:T(8,128)(2,1)S(1)}, u32[]{:S(2)}, u32[]{:S(2)}) collective-permute-start(bf16[832,256]{1,0:T(8,128)(2,1)S(1)} %bitcast.129), channel_id=1, source_target_pairs={{0,128},{64,192},{128,0},{192,64},{1,129},{65,193},{129,1},{193,65... | collective-permute-start | bytes 1277960 | tf_op jit(solution)/shard_map/ppermute | solution.py:15
  80.9 17.7 %collective-permute-start.8 = (bf16[832,256]{1,0:T(8,128)(2,1)S(1)}, bf16[832,256]{1,0:T(8,128)(2,1)S(1)}, u32[]{:S(2)}, u32[]{:S(2)}) collective-permute-start(bf16[832,256]{1,0:T(8,128)(2,1)S(1)} %bitcast.130), channel_id=1, source_target_pairs={{0,64},{64,128},{128,192},{192,0},{1,65},{65,129},{129,193},{193,1... | collective-permute-start | bytes 1277960 | tf_op jit(solution)/shard_map/ppermute | solution.py:15
  82.3 16.3 %collective-permute-start.9 = (bf16[832,256]{1,0:T(8,128)(2,1)S(1)}, bf16[832,256]{1,0:T(8,128)(2,1)S(1)}, u32[]{:S(2)}, u32[]{:S(2)}) collective-permute-start(bf16[832,256]{1,0:T(8,128)(2,1)S(1)} %bitcast.131), channel_id=1, source_target_pairs={{0,192},{64,0},{128,64},{192,128},{1,193},{65,1},{129,65},{193,129... | collective-permute-start | bytes 1277960 | tf_op jit(solution)/shard_map/ppermute | solution.py:15
  102.9 1.9 collective-permute-start.10
  104.9 6.8 %collective-permute-start.11 = (f32[104,256]{1,0:T(8,128)S(1)}, f32[104,256]{1,0:T(8,128)S(1)}, u32[]{:S(2)}, u32[]{:S(2)}) collective-permute-start(f32[104,256]{1,0:T(8,128)S(1)} %get-tuple-element.16), channel_id=1, source_target_pairs={{0,4},{2,6},{4,0},{6,2},{1,5},{3,7},{5,1},{7,3},{8,12},{10,14},{12... | collective-permute-start | bytes 319496 | tf_op jit(solution)/shard_map/ppermute | solution.py:15
  107.2 6.7 %collective-permute-start.12 = (f32[104,256]{1,0:T(8,128)S(1)}, f32[104,256]{1,0:T(8,128)S(1)}, u32[]{:S(2)}, u32[]{:S(2)}) collective-permute-start(f32[104,256]{1,0:T(8,128)S(1)} %get-tuple-element.18), channel_id=1, source_target_pairs={{0,2},{2,4},{4,6},{6,0},{1,3},{3,5},{5,7},{7,1},{8,10},{10,12},{12... | collective-permute-start | bytes 319496 | tf_op jit(solution)/shard_map/ppermute | solution.py:15
  107.9 6.0 %collective-permute-start.13 = (f32[104,256]{1,0:T(8,128)S(1)}, f32[104,256]{1,0:T(8,128)S(1)}, u32[]{:S(2)}, u32[]{:S(2)}) collective-permute-start(f32[104,256]{1,0:T(8,128)S(1)} %get-tuple-element.17), channel_id=1, source_target_pairs={{0,6},{2,0},{4,2},{6,4},{1,7},{3,1},{5,3},{7,5},{8,14},{10,8},{12,... | collective-permute-start | bytes 319496 | tf_op jit(solution)/shard_map/ppermute | solution.py:15
  159.1 13.8 %collective-permute-start.14 = (bf16[832,256]{1,0:T(8,128)(2,1)S(1)}, bf16[832,256]{1,0:T(8,128)(2,1)S(1)}, u32[]{:S(2)}, u32[]{:S(2)}) collective-permute-start(bf16[832,256]{1,0:T(8,128)(2,1)S(1)} %bitcast.125), channel_id=1, source_target_pairs={{0,128},{64,192},{128,0},{192,64},{1,129},{65,193},{129,1},{193,65... | collective-permute-start | bytes 1277960 | tf_op jit(solution)/shard_map/ppermute | solution.py:15
  160.7 16.6 %collective-permute-start.15 = (bf16[832,256]{1,0:T(8,128)(2,1)S(1)}, bf16[832,256]{1,0:T(8,128)(2,1)S(1)}, u32[]{:S(2)}, u32[]{:S(2)}) collective-permute-start(bf16[832,256]{1,0:T(8,128)(2,1)S(1)} %bitcast.126), channel_id=1, source_target_pairs={{0,64},{64,128},{128,192},{192,0},{1,65},{65,129},{129,193},{193,1... | collective-permute-start | bytes 1277960 | tf_op jit(solution)/shard_map/ppermute | solution.py:15
  161.2 16.2 %collective-permute-start.16 = (bf16[832,256]{1,0:T(8,128)(2,1)S(1)}, bf16[832,256]{1,0:T(8,128)(2,1)S(1)}, u32[]{:S(2)}, u32[]{:S(2)}) collective-permute-start(bf16[832,256]{1,0:T(8,128)(2,1)S(1)} %bitcast.127), channel_id=1, source_target_pairs={{0,192},{64,0},{128,64},{192,128},{1,193},{65,1},{129,65},{193,129... | collective-permute-start | bytes 1277960 | tf_op jit(solution)/shard_map/ppermute | solution.py:15
  181.7 1.9 collective-permute-start.17
  183.6 36.5 %copy-start.1 = (bf16[104,256]{1,0:T(8,128)(2,1)S(1)}, bf16[104,256]{1,0:T(8,128)(2,1)}, u32[]{:S(2)}) copy-start(bf16[104,256]{1,0:T(8,128)(2,1)} %param.7) | copy-start | bytes 159748
  183.7 7.4 %collective-permute-start.18 = (f32[104,256]{1,0:T(8,128)S(1)}, f32[104,256]{1,0:T(8,128)S(1)}, u32[]{:S(2)}, u32[]{:S(2)}) collective-permute-start(f32[104,256]{1,0:T(8,128)S(1)} %get-tuple-element.13), channel_id=1, source_target_pairs={{0,4},{2,6},{4,0},{6,2},{1,5},{3,7},{5,1},{7,3},{8,12},{10,14},{12... | collective-permute-start | bytes 319496 | tf_op jit(solution)/shard_map/ppermute | solution.py:15
  184.7 7.8 %collective-permute-start.19 = (f32[104,256]{1,0:T(8,128)S(1)}, f32[104,256]{1,0:T(8,128)S(1)}, u32[]{:S(2)}, u32[]{:S(2)}) collective-permute-start(f32[104,256]{1,0:T(8,128)S(1)} %get-tuple-element.15), channel_id=1, source_target_pairs={{0,2},{2,4},{4,6},{6,0},{1,3},{3,5},{5,7},{7,1},{8,10},{10,12},{12... | collective-permute-start | bytes 319496 | tf_op jit(solution)/shard_map/ppermute | solution.py:15
  185.8 6.8 %collective-permute-start.20 = (f32[104,256]{1,0:T(8,128)S(1)}, f32[104,256]{1,0:T(8,128)S(1)}, u32[]{:S(2)}, u32[]{:S(2)}) collective-permute-start(f32[104,256]{1,0:T(8,128)S(1)} %get-tuple-element.14), channel_id=1, source_target_pairs={{0,6},{2,0},{4,2},{6,4},{1,7},{3,1},{5,3},{7,5},{8,14},{10,8},{12,... | collective-permute-start | bytes 319496 | tf_op jit(solution)/shard_map/ppermute | solution.py:15

commit v3 on v2

v3 whole, which is shorter than its diff:
```python
import jax
import jax.numpy as jnp
from jax import lax
from jax.sharding import Mesh, PartitionSpec as P

Y, ZS, ZP, X, CORE = 4, 4, 2, 4, 2
BF16, F32 = jnp.bfloat16, jnp.float32
ROUNDING, ALLOWED = 8e-4, 8.5e-3


def spread(block, axes, size):
    return lax.all_to_all(jnp.broadcast_to(block[None], (size,) + block.shape), axes, 0, 0, tiled=True)


def gather_rows(block):
    strided = spread(block, "zs", ZS)
    whole = spread(strided, ("y", "zp"), Y * ZP)
    whole = whole.reshape((Y, ZP, ZS) + block.shape).transpose(0, 2, 1, 3, 4)
    return whole.reshape((Y * ZS * ZP,) + block.shape)


def moved(block, axis, size, shift):
    return lax.ppermute(block, axis, [(i, (i + shift) % size) for i in range(size)])


def scatter_rows(partial_sum):
    core = lax.axis_index("core")
    place = lax.axis_index("x")
    split = partial_sum.reshape((X, CORE) + partial_sum.shape[1:])
    mine = lax.dynamic_index_in_dim(split, core, 1, keepdims=False)
    other = lax.dynamic_index_in_dim(split, 1 - core, 1, keepdims=False)
    half = mine + lax.ppermute(other, "core", [(0, 1), (1, 0)])
    total = lax.dynamic_index_in_dim(half, place, 0, keepdims=False)
    for shift in (2, 1, 3):
        total = total + moved(lax.dynamic_index_in_dim(half, (place + shift) % X, 0, keepdims=False), "x", X, shift)
    return total


def total_sums(rows):
    sums = jnp.stack([jnp.sum(first * second, axis=0) for first, second in rows])
    sums = jnp.pad(sums, ((0, 8 - len(rows)), (0, 0)))
    sums = jnp.sum(spread(sums, ("x", "core"), X * CORE), axis=0)
    return jnp.sum(spread(sums, ("y", "zs", "zp"), Y * ZS * ZP), axis=0)


def on_device(hessian, exponents, masks, weights):
    row_scale = jnp.exp2(-exponents.astype(F32))[:, None]
    kept = masks.astype(F32)
    dense = weights.astype(F32)
    rows = exponents.shape[0]

    def product(gathered):
        gathered = gathered.reshape(-1, gathered.shape[-1])
        return jnp.einsum("cst,tk->csk", hessian, gathered, preferred_element_type=F32)

    def owned(partial_sum):
        return kept * row_scale * scatter_rows(partial_sum)

    start = lax.axis_index(("y", "zs", "zp")) * rows
    own_rows = lax.dynamic_index_in_dim(hessian, lax.axis_index(("x", "core")), 0, keepdims=False)
    on_diagonal = lax.broadcasted_iota(jnp.int32, own_rows.shape, 1) == start + lax.broadcasted_iota(
        jnp.int32, own_rows.shape, 0
    )
    diagonal = jnp.sum(jnp.where(on_diagonal, own_rows.astype(F32), 0.0), axis=1, keepdims=True)

    v0 = owned(product(gather_rows((row_scale * ((1.0 - kept) * dense)).astype(BF16))))

    scaled = row_scale * v0
    tail = jnp.stack([jnp.sum(diagonal * scaled * scaled, axis=0), jnp.sum(v0 * v0, axis=0)])
    tail = jnp.pad(tail, ((0, 6), (0, 0)))
    gathered = gather_rows(jnp.concatenate([scaled, tail]).astype(BF16))
    tails = jnp.sum(gathered[:, rows : rows + 2].astype(F32), axis=0)
    shift = jnp.where(tails[1] > 0.0, tails[0] / tails[1], 0.0)
    partial_0 = product(gathered[:, :rows])
    v1 = owned(partial_0)

    partial_1 = product(gather_rows((row_scale * (v1 - shift * v0)).astype(BF16)))
    v2 = owned(partial_1 + shift * partial_0)

    g00, g01, g11, g02, g12, g22, h1, h2 = total_sums(
        [(v0, v0), (v0, v1), (v1, v1), (v0, v2), (v1, v2), (v2, v2), (v0, shift * v0), (shift * v0, shift * v0)]
    )
    step_0 = g00 / g01
    residual = v0 - step_0 * v1
    fresh = g00 - 2.0 * step_0 * g01 + step_0 * step_0 * g11
    ahead = 1.0 + fresh / g00
    along = ahead * ahead * g01 - ahead * step_0 * (g02 + g11) + step_0 * step_0 * g12
    step_1 = fresh / along

    direction_sq = ahead * ahead * g00 - 2.0 * ahead * step_0 * g01 + step_0 * step_0 * g11
    left_sq = ahead * ahead * g00 - 2.0 * ahead * step_0 * h1 + step_0 * step_0 * h2
    with_image = ahead * g01 - step_0 * (g02 + ahead * g11) + step_0 * step_0 * g12
    image_sq = ahead * ahead * g11 - 2.0 * ahead * step_0 * g12 + step_0 * step_0 * g22
    last_sq = fresh - 2.0 * step_1 * with_image + step_1 * step_1 * image_sq
    spread_sq = left_sq + direction_sq + (jnp.sqrt(left_sq) + jnp.sqrt(direction_sq)) ** 2
    error_sq = ROUNDING**2 * jnp.sum(step_1 * step_1 * (g11 / g00) * spread_sq)
    close = error_sq < ALLOWED**2 * jnp.sum(last_sq)

    def short():
        direction = ahead * v0 - step_0 * v1
        image = ahead * v1 - step_0 * v2
        return (kept * dense + step_0 * v0 + step_1 * direction, residual - step_1 * image)

    def long():
        fresh = total_sums([(residual, residual)])[0]
        direction = residual + fresh / g00 * v0
        image = owned(product(gather_rows((row_scale * direction).astype(BF16))))
        step = fresh / total_sums([(direction, image)])[0]
        return (kept * dense + step_0 * v0 + step * direction, residual - step * image)

    return lax.cond(close, short, long)


def solution(mesh):
    fine = Mesh(mesh.devices.reshape(Y, ZS, ZP, X, CORE), ("y", "zs", "zp", "x", "core"))
    row = ("y", "zs", "zp")
    owner = ("x", "core") + row
    in_specs = (P(None, row, ("x", "core")), P(owner), P(owner, None), P(owner, None))
    out_specs = (P(owner, None), P(owner, None))
    return jax.shard_map(on_device, mesh=fine, in_specs=in_specs, out_specs=out_specs, check_vma=False)
```

time: 221 us -> 196 us (0.89)
  blocking collectives: 112 us -> 98.6 us
  starting transfers between devices: 33.2 us -> 24.3 us
  matrix products: 12.6 us -> 7.38 us
  waiting for transfers between devices: 57.6 us -> 54 us
    ppermute x18 -> x9, waiting for transfers between devices: 52.4 us -> 16.8 us  [moved(): lax.ppermute(block, axis, [(i, (i + shift) % size) for i in range(size)])]
    all_to_all x0 -> x2, waiting for transfers between devices: none -> 32 us  [spread(): lax.all_to_all(jnp.broadcast_to(block[None], (size,) + block.shape), axes...]
    ppermute x18 -> x9, starting transfers between devices: 32.9 us -> 12.1 us  [moved(): lax.ppermute(block, axis, [(i, (i + shift) % size) for i in range(size)])]
    all_to_all x7 -> x6, blocking collectives: 112 us -> 98.6 us  [spread(): lax.all_to_all(jnp.broadcast_to(block[None], (size,) + block.shape), axes...]
    all_to_all x0 -> x2, starting transfers between devices: none -> 12 us  [spread(): lax.all_to_all(jnp.broadcast_to(block[None], (size,) + block.shape), axes...]
    dot_general x3, matrix products: 12.6 us -> 7.38 us  [product(): jnp.einsum('cst,tk->csk', hessian, gathered, preferred_element_type=F32)]
  transfers between devices with their start and end apart: 21 -> 14, of which waited for: 16 -> 10; matrix products, arithmetic and copies ran while one was open for 0% -> 1% of each run, Pallas kernels for 0% -> 0%
where the time goes in v3:
time: 196 us; the launch traced here: 195 us
  blocking collectives  98.6 us (50%)
  waiting for transfers between devices  54 us (28%)
  starting transfers between devices  24.3 us (12%)
  matrix products  7.38 us (4%)
  other arithmetic  5.39 us (3%)
  local copies, waits for them, and re-layouts  3.19 us (2%)
  between operations  2.32 us (1%)
    all_to_all x6, blocking collectives, spread(): lax.all_to_all(jnp.broadcast_to(block[None], (size,) + block.shape), axes...  98.6 us
    all_to_all x2, waiting for transfers between devices, spread(): lax.all_to_all(jnp.broadcast_to(block[None], (size,) + block.shape), axes...  32 us
    ppermute x9, waiting for transfers between devices, moved(): lax.ppermute(block, axis, [(i, (i + shift) % size) for i in range(size)])  16.8 us
    ppermute x9, starting transfers between devices, moved(): lax.ppermute(block, axis, [(i, (i + shift) % size) for i in range(size)])  12.1 us
    all_to_all x2, starting transfers between devices, spread(): lax.all_to_all(jnp.broadcast_to(block[None], (size,) + block.shape), axes...  12 us
    dot_general x3, matrix products, product(): jnp.einsum('cst,tk->csk', hessian, gathered, preferred_element_type=F32)  7.38 us
    ppermute x3, waiting for transfers between devices, scatter_rows(): half = mine + lax.ppermute(other, 'core', [(0, 1), (1, 0)])  5.15 us
  transfers between devices with their start and end apart: 14, of which 10 were waited for; matrix products, arithmetic and copies ran while one was open for 1% of the time, Pallas kernels for 0%

profile of v3, /device:TPU:32, one launch (start us, length us, event | category | flops | bytes accessed | tf_op | source)
XLA Modules:
  0.0 195.3 jit_solution(5565449351705100351)
XLA Ops:
  2.3 17.5 %all_to_all.69 = bf16[4,104,256]{2,1,0:T(8,128)(2,1)S(1)} all-to-all(bf16[4,104,256]{2,1,0:T(8,128)(2,1)S(1)} %broadcast_in_dim.35), channel_id=1, replica_groups=mesh['y'=4,'zs'=4,'zp'=2,'x'=4,'core'=2] {'zs'}, dimensions={0} | all-to-all | bytes 425984 | tf_op jit(solution)/shard_map/all_to_all | solution.py:12
  21.1 5.9 %all-to-all-start.7 = ((bf16[8,4,104,256]{3,2,1,0:T(8,128)(2,1)}), bf16[8,4,104,256]{3,2,1,0:T(8,128)(2,1)S(1)}, u32[]{:S(2)}, u32[]{:S(2)}) async-start(bf16[8,4,104,256]{3,2,1,0:T(8,128)(2,1)} %broadcast_in_dim.36), calls=%async_computation.7 | async-start | bytes 3407872 | tf_op jit(solution)/shard_map/all_to_all | solution.py:12
  27.0 19.9 %all-to-all-done.7 = bf16[8,4,104,256]{3,2,1,0:T(8,128)(2,1)S(1)} async-done(((bf16[8,4,104,256]{3,2,1,0:T(8,128)(2,1)}), bf16[8,4,104,256]{3,2,1,0:T(8,128)(2,1)S(1)}, u32[]{:S(2)}, u32[]{:S(2)}) %all-to-all-start.7) | async-done | bytes 1703968 | tf_op jit(solution)/shard_map/all_to_all | solution.py:12
  47.0 4.2 %fusion.27 = f32[256,8,104]{0,2,1:T(8,128)S(1)} fusion(bf16[3328,256,1]{1,0,2:T(8,128)(2,1)S(1)} %bitcast.158, bf16[8,104,3328]{2,1,0:T(8,128)(2,1)} %param.6), kind=kOutput, calls=%fused_computation.89 | convolution fusion | flops 1417674752 | bytes 8093696 | tf_op jit(solution)/shard_map/cst,tk->csk/dot_general | solution.py:54
  51.4 1.7 collective-permute-done.4
  53.2 2.8 %collective-permute-start.7 = (f32[104,256]{1,0:T(8,128)S(1)}, f32[104,256]{1,0:T(8,128)S(1)}, u32[]{:S(2)}, u32[]{:S(2)}) collective-permute-start(f32[104,256]{1,0:T(8,128)S(1)} %get-tuple-element.98), channel_id=1, source_target_pairs={{0,6},{2,0},{4,2},{6,4},{1,7},{3,1},{5,3},{7,5},{8,14},{10,8},{12,... | collective-permute-start | bytes 319496 | tf_op jit(solution)/shard_map/ppermute | solution.py:23
  56.1 2.3 %collective-permute-start.5 = (f32[104,256]{1,0:T(8,128)S(1)}, f32[104,256]{1,0:T(8,128)S(1)}, u32[]{:S(2)}, u32[]{:S(2)}) collective-permute-start(f32[104,256]{1,0:T(8,128)S(1)} %get-tuple-element.97), channel_id=1, source_target_pairs={{0,4},{2,6},{4,0},{6,2},{1,5},{3,7},{5,1},{7,3},{8,12},{10,14},{12... | collective-permute-start | bytes 319496 | tf_op jit(solution)/shard_map/ppermute | solution.py:23
  59.8 4.5 %collective-permute-done.6 = f32[104,256]{1,0:T(8,128)S(1)} collective-permute-done((f32[104,256]{1,0:T(8,128)S(1)}, f32[104,256]{1,0:T(8,128)S(1)}, u32[]{:S(2)}, u32[]{:S(2)}) %collective-permute-start.6) | collective-permute-done | bytes 106528 | tf_op jit(solution)/shard_map/ppermute | solution.py:23
  64.6 13.4 %all_to_all.70 = bf16[4,112,256]{2,1,0:T(8,128)(2,1)S(1)} all-to-all(bf16[4,112,256]{2,1,0:T(8,128)(2,1)S(1)} %broadcast_in_dim.38), channel_id=1, replica_groups=mesh['y'=4,'zs'=4,'zp'=2,'x'=4,'core'=2] {'zs'}, dimensions={0} | all-to-all | bytes 458752 | tf_op jit(solution)/shard_map/all_to_all | solution.py:12
  78.2 24.2 %all_to_all.71 = bf16[8,4,112,256]{3,2,1,0:T(8,128)(2,1)S(1)} all-to-all(bf16[8,4,112,256]{3,2,1,0:T(8,128)(2,1)S(1)} %broadcast_in_dim.39), channel_id=1, replica_groups=mesh['y'=4,'zs'=4,'zp'=2,'x'=4,'core'=2] {'y','zp'}, dimensions={0} | all-to-all | bytes 3670016 | tf_op jit(solution)/shard_map/all_to_all | solution.py:12
  104.5 1.7 collective-permute-done.8
  106.7 1.7 collective-permute-start.10
  108.8 3.0 %collective-permute-done.11 = f32[104,256]{1,0:T(8,128)S(1)} collective-permute-done((f32[104,256]{1,0:T(8,128)S(1)}, f32[104,256]{1,0:T(8,128)S(1)}, u32[]{:S(2)}, u32[]{:S(2)}) %collective-permute-start.11) | collective-permute-done | bytes 106528 | tf_op jit(solution)/shard_map/ppermute | solution.py:23
  111.8 3.2 %collective-permute-done.10 = f32[104,256]{1,0:T(8,128)S(1)} collective-permute-done((f32[104,256]{1,0:T(8,128)S(1)}, f32[104,256]{1,0:T(8,128)S(1)}, u32[]{:S(2)}, u32[]{:S(2)}) %collective-permute-start.10) | collective-permute-done | bytes 106528 | tf_op jit(solution)/shard_map/ppermute | solution.py:23
  115.1 13.4 %all_to_all.72 = bf16[4,104,256]{2,1,0:T(8,128)(2,1)S(1)} all-to-all(bf16[4,104,256]{2,1,0:T(8,128)(2,1)S(1)} %broadcast_in_dim.40), channel_id=1, replica_groups=mesh['y'=4,'zs'=4,'zp'=2,'x'=4,'core'=2] {'zs'}, dimensions={0} | all-to-all | bytes 425984 | tf_op jit(solution)/shard_map/all_to_all | solution.py:12
  128.6 22.1 %all_to_all.73 = bf16[8,4,104,256]{3,2,1,0:T(8,128)(2,1)S(1)} all-to-all(bf16[8,4,104,256]{3,2,1,0:T(8,128)(2,1)S(1)} %broadcast_in_dim.41), channel_id=1, replica_groups=mesh['y'=4,'zs'=4,'zp'=2,'x'=4,'core'=2] {'y','zp'}, dimensions={0} | all-to-all | bytes 3407872 | tf_op jit(solution)/shard_map/all_to_all | solution.py:12
  150.9 1.6 fusion.4
  152.7 1.8 collective-permute-done.12
  154.6 2.5 %collective-permute-start.15 = (f32[104,256]{1,0:T(8,128)S(1)}, f32[104,256]{1,0:T(8,128)S(1)}, u32[]{:S(2)}, u32[]{:S(2)}) collective-permute-start(f32[104,256]{1,0:T(8,128)S(1)} %get-tuple-element.92), channel_id=1, source_target_pairs={{0,6},{2,0},{4,2},{6,4},{1,7},{3,1},{5,3},{7,5},{8,14},{10,8},{12,... | collective-permute-start | bytes 319496 | tf_op jit(solution)/shard_map/ppermute | solution.py:23
  157.0 2.0 %collective-permute-start.13 = (f32[104,256]{1,0:T(8,128)S(1)}, f32[104,256]{1,0:T(8,128)S(1)}, u32[]{:S(2)}, u32[]{:S(2)}) collective-permute-start(f32[104,256]{1,0:T(8,128)S(1)} %get-tuple-element.91), channel_id=1, source_target_pairs={{0,4},{2,6},{4,0},{6,2},{1,5},{3,7},{5,1},{7,3},{8,12},{10,14},{12... | collective-permute-start | bytes 319496 | tf_op jit(solution)/shard_map/ppermute | solution.py:23
  159.6 5.6 %collective-permute-done.14 = f32[104,256]{1,0:T(8,128)S(1)} collective-permute-done((f32[104,256]{1,0:T(8,128)S(1)}, f32[104,256]{1,0:T(8,128)S(1)}, u32[]{:S(2)}, u32[]{:S(2)}) %collective-permute-start.14) | collective-permute-done | bytes 106528 | tf_op jit(solution)/shard_map/ppermute | solution.py:23
  165.4 8.0 %all_to_all.74 = f32[8,8,256]{2,1,0:T(8,128)S(1)} all-to-all(f32[8,8,256]{2,1,0:T(8,128)S(1)} %broadcast_in_dim.42), channel_id=1, replica_groups=mesh['y'=4,'zs'=4,'zp'=2,'x'=4,'core'=2] {'x','core'}, dimensions={0} | all-to-all | bytes 131072 | tf_op jit(solution)/shard_map/all_to_all | solution.py:12
  174.1 6.0 %all-to-all-start.13 = ((f32[32,8,256]{2,1,0:T(8,128)}), f32[32,8,256]{2,1,0:T(8,128)S(1)}, u32[]{:S(2)}, u32[]{:S(2)}) async-start(f32[32,8,256]{2,1,0:T(8,128)} %broadcast_in_dim.43), calls=%async_computation.13 | async-start | bytes 524288 | tf_op jit(solution)/shard_map/all_to_all | solution.py:12
  180.2 12.1 %all-to-all-done.13 = f32[32,8,256]{2,1,0:T(8,128)S(1)} async-done(((f32[32,8,256]{2,1,0:T(8,128)}), f32[32,8,256]{2,1,0:T(8,128)S(1)}, u32[]{:S(2)}, u32[]{:S(2)}) %all-to-all-start.13) | async-done | bytes 262176 | tf_op jit(solution)/shard_map/all_to_all | solution.py:12
  (72 shorter events, 11.9 us)
Async XLA Ops:
  21.1 25.8 %all-to-all-start.7 = ((bf16[8,4,104,256]{3,2,1,0:T(8,128)(2,1)}), bf16[8,4,104,256]{3,2,1,0:T(8,128)(2,1)S(1)}, u32[]{:S(2)}, u32[]{:S(2)}) async-start(bf16[8,4,104,256]{3,2,1,0:T(8,128)(2,1)} %broadcast_in_dim.36), calls=%async_computation.7 | async-start | bytes 3407872 | tf_op jit(solution)/shard_map/all_to_all | solution.py:12
  51.2 13.1 %copy-start = (s32[104,256]{1,0:T(8,128)S(1)}, s32[104,256]{1,0:T(8,128)}, u32[]{:S(2)}) copy-start(s32[104,256]{1,0:T(8,128)} %param.8) | copy-start | bytes 319492
  51.3 1.9 collective-permute-start.4
  53.2 6.6 %collective-permute-start.7 = (f32[104,256]{1,0:T(8,128)S(1)}, f32[104,256]{1,0:T(8,128)S(1)}, u32[]{:S(2)}, u32[]{:S(2)}) collective-permute-start(f32[104,256]{1,0:T(8,128)S(1)} %get-tuple-element.98), channel_id=1, source_target_pairs={{0,6},{2,0},{4,2},{6,4},{1,7},{3,1},{5,3},{7,5},{8,14},{10,8},{12,... | collective-permute-start | bytes 319496 | tf_op jit(solution)/shard_map/ppermute | solution.py:23
  56.1 8.2 %collective-permute-start.6 = (f32[104,256]{1,0:T(8,128)S(1)}, f32[104,256]{1,0:T(8,128)S(1)}, u32[]{:S(2)}, u32[]{:S(2)}) collective-permute-start(f32[104,256]{1,0:T(8,128)S(1)} %get-tuple-element.99), channel_id=1, source_target_pairs={{0,2},{2,4},{4,6},{6,0},{1,3},{3,5},{5,7},{7,1},{8,10},{10,12},{12... | collective-permute-start | bytes 319496 | tf_op jit(solution)/shard_map/ppermute | solution.py:23
  56.1 8.2 %collective-permute-start.5 = (f32[104,256]{1,0:T(8,128)S(1)}, f32[104,256]{1,0:T(8,128)S(1)}, u32[]{:S(2)}, u32[]{:S(2)}) collective-permute-start(f32[104,256]{1,0:T(8,128)S(1)} %get-tuple-element.97), channel_id=1, source_target_pairs={{0,4},{2,6},{4,0},{6,2},{1,5},{3,7},{5,1},{7,3},{8,12},{10,14},{12... | collective-permute-start | bytes 319496 | tf_op jit(solution)/shard_map/ppermute | solution.py:23
  64.3 38.4 %slice-start = ((s8[5537792]{0:T(1024)(128)(4,1)}), s8[4194304]{0:T(1024)(128)(4,1)S(1)}, s32[]{:S(2)}) async-start(s8[5537792]{0:T(1024)(128)(4,1)} %bitcast.169), calls=%async_computation.14 | async-start | bytes 8388608
  78.1 24.5 %slice-start.1 = ((s8[5537792]{0:T(1024)(128)(4,1)}), s8[1343488]{0:T(1024)(128)(4,1)S(1)}, s32[]{:S(2)}) async-start(s8[5537792]{0:T(1024)(128)(4,1)} %bitcast.169), calls=%async_computation.15 | async-start | bytes 2686976
  104.3 1.9 collective-permute-start.8
  106.3 5.5 %collective-permute-start.11 = (f32[104,256]{1,0:T(8,128)S(1)}, f32[104,256]{1,0:T(8,128)S(1)}, u32[]{:S(2)}, u32[]{:S(2)}) collective-permute-start(f32[104,256]{1,0:T(8,128)S(1)} %get-tuple-element.95), channel_id=1, source_target_pairs={{0,6},{2,0},{4,2},{6,4},{1,7},{3,1},{5,3},{7,5},{8,14},{10,8},{12,... | collective-permute-start | bytes 319496 | tf_op jit(solution)/shard_map/ppermute | solution.py:23
  106.7 8.3 %collective-permute-start.10 = (f32[104,256]{1,0:T(8,128)S(1)}, f32[104,256]{1,0:T(8,128)S(1)}, u32[]{:S(2)}, u32[]{:S(2)}) collective-permute-start(f32[104,256]{1,0:T(8,128)S(1)} %get-tuple-element.96), channel_id=1, source_target_pairs={{0,2},{2,4},{4,6},{6,0},{1,3},{3,5},{5,7},{7,1},{8,10},{10,12},{12... | collective-permute-start | bytes 319496 | tf_op jit(solution)/shard_map/ppermute | solution.py:23
  108.4 6.6 %collective-permute-start.9 = (f32[104,256]{1,0:T(8,128)S(1)}, f32[104,256]{1,0:T(8,128)S(1)}, u32[]{:S(2)}, u32[]{:S(2)}) collective-permute-start(f32[104,256]{1,0:T(8,128)S(1)} %get-tuple-element.94), channel_id=1, source_target_pairs={{0,4},{2,6},{4,0},{6,2},{1,5},{3,7},{5,1},{7,3},{8,12},{10,14},{12... | collective-permute-start | bytes 319496 | tf_op jit(solution)/shard_map/ppermute | solution.py:23
  152.6 1.9 collective-permute-start.12
  154.5 25.7 %copy-start.1 = (bf16[104,256]{1,0:T(8,128)(2,1)S(1)}, bf16[104,256]{1,0:T(8,128)(2,1)}, u32[]{:S(2)}) copy-start(bf16[104,256]{1,0:T(8,128)(2,1)} %param.9) | copy-start | bytes 159748
  154.6 5.1 %collective-permute-start.15 = (f32[104,256]{1,0:T(8,128)S(1)}, f32[104,256]{1,0:T(8,128)S(1)}, u32[]{:S(2)}, u32[]{:S(2)}) collective-permute-start(f32[104,256]{1,0:T(8,128)S(1)} %get-tuple-element.92), channel_id=1, source_target_pairs={{0,6},{2,0},{4,2},{6,4},{1,7},{3,1},{5,3},{7,5},{8,14},{10,8},{12,... | collective-permute-start | bytes 319496 | tf_op jit(solution)/shard_map/ppermute | solution.py:23
  157.0 8.2 %collective-permute-start.14 = (f32[104,256]{1,0:T(8,128)S(1)}, f32[104,256]{1,0:T(8,128)S(1)}, u32[]{:S(2)}, u32[]{:S(2)}) collective-permute-start(f32[104,256]{1,0:T(8,128)S(1)} %get-tuple-element.93), channel_id=1, source_target_pairs={{0,2},{2,4},{4,6},{6,0},{1,3},{3,5},{5,7},{7,1},{8,10},{10,12},{12... | collective-permute-start | bytes 319496 | tf_op jit(solution)/shard_map/ppermute | solution.py:23
  157.0 8.2 %collective-permute-start.13 = (f32[104,256]{1,0:T(8,128)S(1)}, f32[104,256]{1,0:T(8,128)S(1)}, u32[]{:S(2)}, u32[]{:S(2)}) collective-permute-start(f32[104,256]{1,0:T(8,128)S(1)} %get-tuple-element.91), channel_id=1, source_target_pairs={{0,4},{2,6},{4,0},{6,2},{1,5},{3,7},{5,1},{7,3},{8,12},{10,14},{12... | collective-permute-start | bytes 319496 | tf_op jit(solution)/shard_map/ppermute | solution.py:23
  174.1 18.2 %all-to-all-start.13 = ((f32[32,8,256]{2,1,0:T(8,128)}), f32[32,8,256]{2,1,0:T(8,128)S(1)}, u32[]{:S(2)}, u32[]{:S(2)}) async-start(f32[32,8,256]{2,1,0:T(8,128)} %broadcast_in_dim.43), calls=%async_computation.13 | async-start | bytes 524288 | tf_op jit(solution)/shard_map/all_to_all | solution.py:12
